TPU v7x, 256 devices: a whole 4x4x8 slice. The times are simulated.
256 devices in a mesh: expert: 8 (over z), shard: 32 (over y, x, core).
Axes of the slice: x: 4, y: 4, z: 8, core: 2. Of those that a mesh axis runs over, the one named last changes fastest.
Arguments:
- tokens: bfloat16 [256, 6144], P('expert'), may hold values from -6 to 6
- routes: int32 [256, 2], P('expert'), may hold values from 0 to 7, all different within a row; in each aligned block of 32 rows (0 to 31, 32 to 63, ...) at most 16 rows name the same one
- router_logits: float32 [256, 2], P('expert'), may hold values from -6 to 6
- gate_weight: bfloat16 [8, 6144, 8192], P('expert', None, 'shard'), may hold values from -0.078125 to 0.078125
- up_weight: bfloat16 [8, 6144, 8192], P('expert', None, 'shard'), may hold values from -0.078125 to 0.078125
- down_weight: bfloat16 [8, 8192, 4096], P('expert', 'shard'), may hold values from -6 to 6
- kept_blocks: int32 [8, 64, 32], P('expert', 'shard'), may hold values 0 or 1
Outputs:
- refit_out: bfloat16 [256, 4096], P('expert', 'shard')
- new_down: bfloat16 [8, 8192, 4096], P('expert', 'shard')
Inputs may be any that keep to these rules, and one draw needn't show every extreme that they name: `routes`: within the 32 rows of one owning group, each expert is named by at most 16 picks, a bound that some block reaches; the two picks of a row differ.
All inputs are finite; a program needn't handle non-finite values. No bound on the sum of `kept_blocks` on one device may be relied on, other than what follows from the above.
Results may differ from a plain program's by a relative error of at most 0.024.
Values may be sent and summed in bfloat16 or wider, within the bound.
A program may use at most 128 MiB of HBM per device.

v0:
```python
import jax
import jax.numpy as jnp
from jax import lax
from jax.sharding import PartitionSpec as P

FF = 8192
BLOCK = 128
ITERS = 3


epsilon = 1e-06


def shortened(value):
    return jax.tree.map(lambda a: a.astype(jnp.bfloat16) if a.dtype == jnp.float32 else a, value)


def expand_mask(blocks, block_edge):
    row_blocks, col_blocks = blocks.shape
    spread = jnp.broadcast_to(
        blocks[:, None, :, None], (row_blocks, block_edge, col_blocks, block_edge)
    )
    return spread.reshape(row_blocks * block_edge, col_blocks * block_edge).astype(jnp.float32)


def slot_targets(routes, experts, capacity):
    chosen = routes.reshape(-1)
    onehot = (chosen[:, None] == jnp.arange(experts, dtype=jnp.int32)[None, :]).astype(jnp.int32)
    before = jnp.cumsum(onehot, axis=0) - onehot
    slot_rank = jnp.sum(before * onehot, axis=1)
    return (chosen * capacity + slot_rank).reshape(routes.shape)


def squared_total(operand):
    return lax.psum(jnp.sum(operand * operand), "shard")


def image_total(operand):
    return lax.psum(jnp.sum(operand * operand), "shard")


def body(tokens, routes, router_logits, gate_weight, up_weight, down_weight, kept_blocks):
    experts = lax.axis_size("expert")
    tok_rows = tokens.shape[0]
    capacity = 4 * tok_rows // experts
    factor = FF ** (-0.5)
    highest = lax.Precision.HIGHEST
    targets = slot_targets(routes, experts, capacity)
    slot_ids = jnp.arange(experts * capacity, dtype=jnp.int32)
    matches = (slot_ids[:, None, None] == targets[None, :, :]).astype(jnp.float32)
    placing = jnp.sum(matches, axis=2).astype(jnp.bfloat16)
    first_share = jax.nn.sigmoid(router_logits[:, 0] - router_logits[:, 1])
    shares = jnp.stack([first_share, 1.0 - first_share], axis=1)
    combining = jnp.sum(matches * shares[None, :, :], axis=2)
    gate_local = gate_weight[0]
    up_local = up_weight[0]
    outgoing = jnp.dot(placing, tokens, preferred_element_type=jnp.float32).astype(jnp.bfloat16)
    arrived = lax.all_to_all(
        outgoing.reshape(experts, capacity, tokens.shape[1]),
        "expert",
        split_axis=0,
        concat_axis=0,
        tiled=True,
    )
    arrived = arrived.reshape(experts * capacity, tokens.shape[1])
    gate_act = jnp.dot(arrived, gate_local, preferred_element_type=jnp.float32)
    up_act = jnp.dot(arrived, up_local, preferred_element_type=jnp.float32)
    hidden = (jax.nn.silu(gate_act) * up_act).astype(jnp.bfloat16)
    keep_mask = expand_mask(kept_blocks[0], BLOCK)
    initial = down_weight[0].astype(jnp.float32)

    def forward(operand):
        terms = factor * jnp.dot(hidden, operand, precision=highest)
        return lax.psum_scatter(
            terms.astype(jnp.bfloat16), "shard", scatter_dimension=1, tiled=True
        ).astype(jnp.float32)

    def adjoint(operand):
        return keep_mask * (
            factor
            * jnp.dot(
                hidden.T,
                lax.all_gather(shortened(operand), "shard", axis=1, tiled=True),
                precision=highest,
            )
        )

    weights = keep_mask * initial
    residual = forward(initial - weights)
    gradient = adjoint(residual)
    direction = gradient
    grad_norm = squared_total(gradient)
    for iteration in range(ITERS):
        image_cols = forward(direction)
        step_size = grad_norm / (image_total(image_cols) + epsilon)
        weights = weights + step_size * direction
        if iteration + 1 < ITERS:
            residual = residual - step_size * image_cols
            gradient = adjoint(residual)
            new_norm = squared_total(gradient)
            direction = gradient + new_norm / (grad_norm + epsilon) * direction
            grad_norm = new_norm
    fitted = forward(weights).astype(jnp.bfloat16)
    returned = lax.all_to_all(
        fitted.reshape(experts, capacity, fitted.shape[1]),
        "expert",
        split_axis=0,
        concat_axis=0,
        tiled=True,
    )
    returned = returned.reshape(experts * capacity, fitted.shape[1]).astype(jnp.float32)
    refit_rows = jnp.dot(combining.T, returned, precision=highest).astype(jnp.bfloat16)
    new_local = weights.astype(jnp.bfloat16)
    return (refit_rows, new_local[None])


def solution(mesh):
    in_specs = (
        P("expert", None),
        P("expert", None),
        P("expert", None),
        P("expert", None, "shard"),
        P("expert", None, "shard"),
        P("expert", "shard", None),
        P("expert", "shard", None),
    )
    out_specs = (P("expert", "shard"), P("expert", "shard", None))
    return jax.shard_map(body, mesh=mesh, in_specs=in_specs, out_specs=out_specs, check_vma=False)
```

profile of v0, /device:TPU:1, one launch (start us, length us, event | category | flops | bytes accessed | tf_op | source)
XLA Modules:
  0.0 1045.6 jit_solution(13342519759990775580)
XLA Ops:
  10.4 2.7 convolution_convert_fusion
  13.1 9.0 all-to-all-start
  22.2 38.3 %all-to-all-done = bf16[8,16,6144]{2,1,0:T(8,128)(2,1)} async-done(((bf16[8,16,6144]{2,1,0:T(8,128)(2,1)}), bf16[8,16,6144]{2,1,0:T(8,128)(2,1)}, u32[]{:S(2)}, u32[]{:S(2)}) %all-to-all-start) | async-done | bytes 1572896 | tf_op jit(solution)/shard_map/all_to_all | solution.py:58
  62.9 2.1 fusion.20
  67.5 5.1 fusion.6
  72.6 2.3 copy.27
  75.0 82.0 %reduce-scatter.16.cloned.1.call-done = bf16[128,128]{1,0:T(8,128)(2,1)} async-done(((bf16[4096,128]{1,0:T(8,128)(2,1)}), bf16[128,128]{1,0:T(8,128)(2,1)}) %reduce-scatter.16.cloned.1.call-update) | async-done | bytes 32784
  158.5 50.7 %all-gather.4.cloned.1.call-done = bf16[128,4096]{1,0:T(8,128)(2,1)} async-done(((bf16[128,128]{1,0:T(8,128)(2,1)}), bf16[128,4096]{1,0:T(8,128)(2,1)}) %all-gather.4.cloned.1.call-update) | async-done | bytes 1048592 | tf_op jit(solution)/shard_map/all_gather | solution.py:83
  209.1 6.1 multiply_reduce_fusion.2
  217.2 2.8 fusion.7
  220.1 2.3 copy.29
  222.5 82.6 %reduce-scatter.18.cloned.1.call-done = bf16[128,128]{1,0:T(8,128)(2,1)} async-done(((bf16[4096,128]{1,0:T(8,128)(2,1)}), bf16[128,128]{1,0:T(8,128)(2,1)}) %reduce-scatter.18.cloned.1.call-update) | async-done | bytes 32784
  306.6 65.1 %all-reduce = (f32[]{:T(128)}, f32[]{:T(128)}) all-reduce(f32[]{:T(128)} %get-tuple-element.10, f32[]{:T(128)} %fusion.23), channel_id=1, replica_groups=mesh['expert'=8,'shard'=32] {'shard'}, use_global_device_ids=true, to_apply=%region_6.7 | all-reduce | flops 2 | bytes 16 | tf_op jit(solution)/shard_map/psum | solution.py:35
  374.4 44.8 %all-gather.6.cloned.1.call-done = bf16[128,4096]{1,0:T(8,128)(2,1)} async-done(((bf16[128,128]{1,0:T(8,128)(2,1)}), bf16[128,4096]{1,0:T(8,128)(2,1)}) %all-gather.6.cloned.1.call-update) | async-done | bytes 1048592 | tf_op jit(solution)/shard_map/all_gather | solution.py:83
  419.2 8.0 multiply_reduce_fusion.1
  427.1 62.9 %psum.44 = f32[]{:T(128)} all-reduce(f32[]{:T(128)} %get-tuple-element.12), channel_id=1, replica_groups=mesh['expert'=8,'shard'=32] {'shard'}, use_global_device_ids=true, to_apply=%region_11.12 | all-reduce | flops 1 | bytes 8 | tf_op jit(solution)/shard_map/psum | solution.py:35
  490.7 6.5 fusion.8
  497.2 2.3 copy.31
  499.6 82.5 %reduce-scatter.20.cloned.1.call-done = bf16[128,128]{1,0:T(8,128)(2,1)} async-done(((bf16[4096,128]{1,0:T(8,128)(2,1)}), bf16[128,128]{1,0:T(8,128)(2,1)}) %reduce-scatter.20.cloned.1.call-update) | async-done | bytes 32784
  583.6 64.9 %psum.45 = f32[]{:T(128)} all-reduce(f32[]{:T(128)} %fusion.25), channel_id=1, replica_groups=mesh['expert'=8,'shard'=32] {'shard'}, use_global_device_ids=true, to_apply=%region_14.15 | all-reduce | flops 1 | bytes 8 | tf_op jit(solution)/shard_map/psum | solution.py:39
  651.2 44.8 %all-gather.8.cloned.1.call-done = bf16[128,4096]{1,0:T(8,128)(2,1)} async-done(((bf16[128,128]{1,0:T(8,128)(2,1)}), bf16[128,4096]{1,0:T(8,128)(2,1)}) %all-gather.8.cloned.1.call-update) | async-done | bytes 1048592 | tf_op jit(solution)/shard_map/all_gather | solution.py:83
  695.9 7.9 multiply_reduce_fusion
  703.9 62.9 %psum.46 = f32[]{:T(128)} all-reduce(f32[]{:T(128)} %get-tuple-element.14), channel_id=1, replica_groups=mesh['expert'=8,'shard'=32] {'shard'}, use_global_device_ids=true, to_apply=%region_16.17 | all-reduce | flops 1 | bytes 8 | tf_op jit(solution)/shard_map/psum | solution.py:35
  767.4 7.9 fusion.9
  775.4 2.3 copy.33
  777.7 82.6 %reduce-scatter.22.cloned.1.call-done = bf16[128,128]{1,0:T(8,128)(2,1)} async-done(((bf16[4096,128]{1,0:T(8,128)(2,1)}), bf16[128,128]{1,0:T(8,128)(2,1)}) %reduce-scatter.22.cloned.1.call-update) | async-done | bytes 32784
  861.8 65.1 %psum.47 = f32[]{:T(128)} all-reduce(f32[]{:T(128)} %multiply_reduce_fusion.3), channel_id=1, replica_groups=mesh['expert'=8,'shard'=32] {'shard'}, use_global_device_ids=true, to_apply=%region_19.20 | all-reduce | flops 1 | bytes 8 | tf_op jit(solution)/shard_map/psum | solution.py:39
  928.2 9.8 convert_bitcast_fusion
  938.1 2.9 fusion.10
  941.0 2.3 copy.35
  943.3 80.5 %reduce-scatter.24.cloned.1.call-done = bf16[128,128]{1,0:T(8,128)(2,1)} async-done(((bf16[4096,128]{1,0:T(8,128)(2,1)}), bf16[128,128]{1,0:T(8,128)(2,1)}) %reduce-scatter.24.cloned.1.call-update) | async-done | bytes 32784
  1024.6 13.4 %all_to_all.10 = bf16[8,16,128]{2,1,0:T(8,128)(2,1)S(1)} all-to-all(bf16[8,16,128]{2,1,0:T(8,128)(2,1)S(1)} %bitcast.80), channel_id=1, replica_groups=mesh['expert'=8,'shard'=32] {'expert'}, dimensions={0} | all-to-all | bytes 65536 | tf_op jit(solution)/shard_map/all_to_all | solution.py:104
  (55 shorter events, 19.3 us)
Async XLA Ops:
  7.2 53.3 %copy-start = (bf16[1,6144,256]{2,1,0:T(8,128)(2,1)S(1)}, bf16[1,6144,256]{2,1,0:T(8,128)(2,1)}, u32[]{:S(2)}) copy-start(bf16[1,6144,256]{2,1,0:T(8,128)(2,1)} %param.10) | copy-start | bytes 9437188
  7.2 15.0 %copy-start.6 = (s32[1,2,32]{2,1,0:T(2,128)S(1)}, s32[1,2,32]{2,1,0:T(2,128)}, u32[]{:S(2)}) copy-start(s32[1,2,32]{2,1,0:T(2,128)} %param.13) | copy-start | bytes 772
  13.1 47.4 %all-to-all-start = ((bf16[8,16,6144]{2,1,0:T(8,128)(2,1)}), bf16[8,16,6144]{2,1,0:T(8,128)(2,1)}, u32[]{:S(2)}, u32[]{:S(2)}) async-start(bf16[8,16,6144]{2,1,0:T(8,128)(2,1)} %bitcast.73), calls=%async_computation | async-start | bytes 3145728 | tf_op jit(solution)/shard_map/all_to_all | solution.py:58
  22.1 134.8 %reduce-scatter.16.cloned.1.call-start = ((), (), s32[]{:S(2)}) async-start(), calls=%async_computation.10 | async-start | bytes 1081344
  60.5 2.4 copy-start.4
  62.9 4.7 copy-start.3
  65.6 1.9 copy-start.1
  74.9 134.2 %all-gather.4.cloned.1.call-start = ((), (), s32[]{:S(2)}) async-start(), calls=%async_computation.7 | async-start | bytes 1081344 | tf_op jit(solution)/shard_map/all_gather | solution.py:83
  158.4 146.7 %reduce-scatter.18.cloned.1.call-start = ((), (), s32[]{:S(2)}) async-start(), calls=%async_computation.11 | async-start | bytes 1081344
  215.3 2.0 copy-start.2
  217.2 155.8 %copy-start.5 = (bf16[128,128]{1,0:T(8,128)(2,1)S(1)}, bf16[128,128]{1,0:T(8,128)(2,1)}, u32[]{:S(2)}) copy-start(bf16[128,128]{1,0:T(8,128)(2,1)} %copy.28) | copy-start | bytes 98308
  222.4 196.7 %all-gather.6.cloned.1.call-start = ((), (), s32[]{:S(2)}) async-start(), calls=%async_computation.8 | async-start | bytes 1081344 | tf_op jit(solution)/shard_map/all_gather | solution.py:83
  373.7 208.4 %reduce-scatter.20.cloned.1.call-start = ((), (), s32[]{:S(2)}) async-start(), calls=%async_computation.12 | async-start | bytes 1081344
  499.5 196.4 %all-gather.8.cloned.1.call-start = ((), (), s32[]{:S(2)}) async-start(), calls=%async_computation.9 | async-start | bytes 1081344 | tf_op jit(solution)/shard_map/all_gather | solution.py:83
  650.5 209.8 %reduce-scatter.22.cloned.1.call-start = ((), (), s32[]{:S(2)}) async-start(), calls=%async_computation.13 | async-start | bytes 1081344
  777.7 246.1 %reduce-scatter.24.cloned.1.call-start = ((), (), s32[]{:S(2)}) async-start(), calls=%async_computation.14 | async-start | bytes 1081344
Sparse Core Ops, SparseCore 0:
  75.0 81.8 reduce-scatter.15
  159.7 49.3 all-gather.3
  222.6 82.4 reduce-scatter.17
  373.8 45.2 all-gather.5
  499.6 82.4 reduce-scatter.19
  650.6 45.2 all-gather.7
  777.8 82.4 reduce-scatter.21
  943.4 80.3 reduce-scatter.23
where the time goes:
time: 1050 us
  waiting for transfers between devices  589 us (56%)
  blocking collectives  334 us (32%)
  matrix products  55 us (5%)
  local copies, waits for them, and re-layouts  22.3 us (2%)
  between operations  20.8 us (2%)
  other arithmetic  15 us (1%)
    unnamed x13, waiting for transfers between devices  410 us
    psum x3, blocking collectives, squared_total(): return lax.psum(jnp.sum(operand * operand), 'shard')  191 us
    all_gather x3, waiting for transfers between devices, adjoint(): lax.all_gather(shortened(operand), 'shard', axis=1, tiled=True)  140 us
    psum x2, blocking collectives, image_total(): return lax.psum(jnp.sum(operand * operand), 'shard')  130 us
    all_to_all x1, waiting for transfers between devices, body(): lax.all_to_all(outgoing.reshape(experts, capacity, tokens.shape[1]), 'exp...  38.3 us
    dot_general x5, matrix products, forward(): terms = factor * jnp.dot(hidden, operand, precision=highest)  25.2 us
    dot_general x3, matrix products, adjoint(): jnp.dot(hidden.T, lax.all_gather(shortened(operand), 'shard', axis=1, til...  22 us
    unnamed x25, local copies, waits for them, and re-layouts  21.4 us
  transfers between devices with their start and end apart: 9, of which 9 were waited for; matrix products, arithmetic and copies ran while one was open for 0% of the time, Pallas kernels for 0%

commit v1 on v0

v1 whole, which is shorter than its diff:
```python
import functools

import jax
import jax.numpy as jnp
from jax import lax
from jax.experimental import pallas as pl
from jax.experimental.pallas import tpu as pltpu
from jax.sharding import PartitionSpec as P

FF = 8192
DW = 4096
EPS = 1e-6
FACTOR = FF ** -0.5
CAP = 16
GROUPS = 8
CHIPS = 16
SHARDS = 32
ROWS = GROUPS * CAP
TINY = 1e-30
MESH = pl.DeviceIdType.MESH
F32 = jnp.float32
BF16 = jnp.bfloat16

ORDER = (1, 3, 5, 7, 0, 2, 4, 6)


def dot(a, b, ca=1, cb=0):
    return lax.dot_general(a, b, (((ca,), (cb,)), ((), ())), preferred_element_type=F32)


def slot_columns(routes_ref, plane):
    rel = [lax.rem(routes_ref[:, k:k + 1] - plane + GROUPS, GROUPS) for k in range(2)]
    tok = rel[0].shape[0]
    lanes = lax.broadcasted_iota(jnp.int32, (tok, 128), 1)
    onehot = [(r == lanes).astype(F32) for r in rel]
    lower = lax.broadcasted_iota(jnp.int32, (tok, tok), 1) < lax.broadcasted_iota(jnp.int32, (tok, tok), 0)
    before = dot(lower.astype(BF16), (onehot[0] + onehot[1]).astype(BF16))
    slots = [jnp.sum(before * o, axis=1, keepdims=True) for o in onehot]
    return [((r * CAP).astype(F32) + s == lanes.astype(F32)) for r, s in zip(rel, slots)]


def step_scalars(m, eps1, eps2):
    def form(p, shift):
        total = None
        size = None
        for i, a in enumerate(p):
            for j, b in enumerate(p):
                term = a * b * m[i + j + shift]
                total = term if total is None else total + term
                size = jnp.abs(term) if size is None else size + jnp.abs(term)
        return jnp.maximum(total, 0.0), size

    one = jnp.ones_like(m[1])
    r, s = [one], [one]
    gnorm, _ = form(r, 1)
    out = None
    for it in range(3):
        image, size = form(s, 2)
        image = jnp.maximum(image, 1e-6 * size)
        step = gnorm / (image + eps2)
        term = [step * a for a in s]
        out = term if out is None else [a + b for a, b in zip(out + [0.0] * (len(term) - len(out)), term)]
        if it < 2:
            r = [a - b for a, b in zip(r + [0.0], [0.0] + term)]
            fresh, _ = form(r, 1)
            beta = fresh / (gnorm + eps1)
            s = [a + b for a, b in zip(r, [beta * c for c in s] + [0.0])]
            gnorm = fresh
    return out


def kernel(tok_hbm, routes_ref, logits_ref, gate_hbm, up_hbm, down_hbm, kept_ref,
           refit_ref, new_ref,
           tok, gate, up, down, outgoing, xg, acc_g, acc_u, hown, hsib, ht, vsib, kb, ksib, gram,
           stage, rs, av, tiles, sg, fit, ret,
           load_sem, z_ssem, z_rsem, ag_ssem, ag_rsem, fw_ssem, fw_rsem, v_ssem, v_rsem, k_sem, h_sem,
           rs_ssem, rs_rsem, av_ssem, av_rsem, t_ssem, t_rsem, s_ssem, s_rsem, sf_ssem, sf_rsem, r_ssem, r_rsem):
    e = lax.axis_index("expert")
    s = lax.axis_index("shard")
    p = s // 2
    c = lax.rem(s, 2)
    sib = (e, 2 * p + 1 - c)
    width = tok.shape[1]

    def chip(k):
        return lax.rem(p + k, CHIPS)

    def from_chip(k):
        return lax.rem(p + CHIPS - k, CHIPS)

    def plane(d):
        return lax.rem(e + d, GROUPS)

    def back(d):
        return lax.rem(e + GROUPS - d, GROUPS)

    def remote(src, dst, ssem, rsem, device):
        return pltpu.make_async_remote_copy(src_ref=src, dst_ref=dst, send_sem=ssem, recv_sem=rsem,
                                            device_id=device, device_id_type=MESH)

    def loop(lo, hi, f):
        lax.fori_loop(lo, hi, lambda k, _: (f(k), 0)[1], 0)

    barrier = pltpu.get_barrier_semaphore()
    loop(1, GROUPS, lambda d: pl.semaphore_signal(barrier, inc=1, device_id=(plane(d), s), device_id_type=MESH))
    loop(1, SHARDS, lambda k: pl.semaphore_signal(barrier, inc=1, device_id=(e, lax.rem(s + k, SHARDS)), device_id_type=MESH))

    loads = [
        pltpu.make_async_copy(tok_hbm.at[:, pl.ds(pl.multiple_of(p * width, 128), width)], tok, load_sem.at[0]),
        pltpu.make_async_copy(gate_hbm.at[0], gate, load_sem.at[1]),
        pltpu.make_async_copy(up_hbm.at[0], up, load_sem.at[2]),
        pltpu.make_async_copy(down_hbm.at[0], down, load_sem.at[3]),
    ]
    for load in loads:
        load.start()

    match = slot_columns(routes_ref, e)
    logit = logits_ref[:, 0:1] - logits_ref[:, 1:2]
    share = 1.0 / (1.0 + jnp.exp(-logit))
    combining = jnp.where(match[0], share, 0.0) + jnp.where(match[1], 1.0 - share, 0.0)
    kept = kept_ref[0].astype(F32)
    row = lax.broadcasted_iota(jnp.int32, (2, 128), 0)
    for f in range(2):
        kb[f] = dot(kept, (row == f).astype(F32), 0, 0)
    loads[0].wait()
    placing = (match[0] | match[1]).astype(BF16)
    outgoing[...] = dot(placing, tok[...], 0, 0).astype(BF16)

    pl.semaphore_wait(barrier, GROUPS - 1 + SHARDS - 1)

    def z_copy(i):
        d = 2 * i + 1 - c
        return remote(outgoing.at[pl.ds(pl.multiple_of(d * CAP, CAP), CAP)],
                      xg.at[p, c, pl.ds(pl.multiple_of(i * CAP, CAP), CAP)],
                      z_ssem.at[i], z_rsem.at[i], (plane(d), s))

    @pl.when(c == 0)
    def _():
        z_copy(0).start()

    @pl.when(c == 1)
    def _():
        xg[p, 1, 0:CAP] = outgoing[0:CAP]

    loop(1, 4, lambda i: z_copy(i).start())

    def v_copy(q):
        return remote(down_hbm.at[0, :, pl.ds(pl.multiple_of((2 * q + 1 - c) * 128, 128), 128)], vsib.at[q],
                      v_ssem.at[q], v_rsem.at[q], sib)

    loop(0, CHIPS, lambda q: v_copy(q).start())
    k_copy = remote(kb, ksib, k_sem.at[0], k_sem.at[1], sib)
    k_copy.start()

    @pl.when(c == 0)
    def _():
        z_copy(0).wait_recv()

    loop(1, 4, lambda i: z_copy(i).wait_recv())

    def ag_copy(k, q):
        return remote(xg.at[q, c], xg.at[q, c], ag_ssem.at[k], ag_rsem.at[k], (e, 2 * chip(k) + c))

    def fw_copy(k, q):
        return remote(xg.at[q, c], xg.at[q, c], fw_ssem.at[k], fw_rsem.at[k], sib)

    def fw_wait(k, q):
        remote(xg.at[q, 1 - c], xg.at[q, 1 - c], fw_ssem.at[k], fw_rsem.at[k], sib).wait_recv()

    loop(1, CHIPS, lambda k: ag_copy(k, p).start())
    fw_copy(0, p).start()
    for load in loads[1:]:
        load.wait()
    acc_g[...] = jnp.zeros_like(acc_g)
    acc_u[...] = jnp.zeros_like(acc_u)

    def expand(k):
        q = from_chip(k)
        fw_wait(k, q)
        x = xg[q].reshape(ROWS, width)
        rows = pl.ds(pl.multiple_of(q * width, 128), width)
        acc_g[...] += dot(x, gate[rows, :])
        acc_u[...] += dot(x, up[rows, :])

    def gather_step(k):
        q = from_chip(k)
        ag_copy(k, q).wait_recv()
        fw_copy(k, q).start()
        expand(k - 1)

    loop(1, CHIPS, gather_step)
    expand(CHIPS - 1)

    g = acc_g[...]
    h32 = g / (1.0 + jnp.exp(-g)) * acc_u[...]
    hown[...] = h32.astype(BF16)
    h_copy = remote(hown, hsib, h_sem.at[0], h_sem.at[1], sib)
    h_copy.start()
    ht[...] = jnp.transpose(hown[...].astype(F32)).astype(BF16)

    def grams(h, base):
        for f in range(2):
            hf = h[:, f * 128:(f + 1) * 128]
            gram[base + f] = FACTOR * FACTOR * dot(hf, hf, 1, 1)

    grams(hown[...], 0)
    loop(0, CHIPS, lambda q: v_copy(q).wait_recv())
    k_copy.wait()
    h_copy.wait()
    grams(hsib[...], 2)

    def masked(v, k0, k1):
        return jnp.concatenate([v[:128] * (1.0 - k0).astype(BF16), v[128:] * (1.0 - k1).astype(BF16)], axis=0)

    def rs_copy(k, q):
        return remote(stage.at[q, pl.ds(0, 2)], rs.at[p], rs_ssem.at[k], rs_rsem.at[k], (e, 2 * q + c))

    def av_copy(k, q):
        return remote(stage.at[q, 2], av.at[p], av_ssem.at[k], av_rsem.at[k], (e, 2 * q + c))

    def partial(q):
        j = 2 * q + c
        ko = [kb[f, pl.ds(j, 1), :] for f in range(2)]
        ks = [ksib[f, pl.ds(j, 1), :] for f in range(2)]
        stage[q, 0] = (ko[0] * gram[0] + ko[1] * gram[1] + ks[0] * gram[2] + ks[1] * gram[3]).astype(BF16)
        vo = down[:, pl.ds(pl.multiple_of(j * 128, 128), 128)]
        vs = vsib[q]
        both = dot(hown[...], jnp.concatenate([masked(vo, *ko), vo], axis=1))
        both += dot(hsib[...], jnp.concatenate([masked(vs, *ks), vs], axis=1))
        both = (FACTOR * both).astype(BF16)
        stage[q, 1] = both[:, :128]
        stage[q, 2] = both[:, 128:]

    def send_partial(k):
        q = chip(k)
        partial(q)
        rs_copy(k, q).start()

    loop(1, CHIPS, send_partial)
    loop(1, CHIPS, lambda k: av_copy(k, chip(k)).start())
    partial(p)

    def add_up(k, carry):
        q = from_chip(k)
        remote(stage.at[p, pl.ds(0, 2)], rs.at[q], rs_ssem.at[k], rs_rsem.at[k], (e, 2 * q + c)).wait_recv()
        return carry[0] + rs[q, 0].astype(F32), carry[1] + rs[q, 1].astype(F32)

    big, r0 = lax.fori_loop(1, CHIPS, add_up, (stage[p, 0].astype(F32), stage[p, 1].astype(F32)))

    eye = lax.broadcasted_iota(jnp.int32, (128, 128), 0) == lax.broadcasted_iota(jnp.int32, (128, 128), 1)
    scale = jnp.sum(jnp.sum(jnp.where(eye, big, 0.0), axis=0, keepdims=True), axis=1, keepdims=True)
    scale = jnp.maximum(scale, TINY)
    mb = (big / scale).astype(BF16)

    def apply(v):
        hi = v.astype(BF16)
        lo = (v - hi.astype(F32)).astype(BF16)
        w = dot(mb, jnp.concatenate([hi, lo], axis=1))
        return w[:, :128] + w[:, 128:]

    v1 = apply(r0)
    v2 = apply(v1)
    v3 = apply(v2)

    def inner(a, b):
        return jnp.sum(a * b, axis=0, keepdims=True)

    tiles[s] = jnp.concatenate(
        [inner(r0, v1), inner(v1, v1), inner(v1, v2), inner(v2, v2), inner(v2, v3), inner(v3, v3),
         jnp.broadcast_to(scale, (1, 128)), jnp.zeros((1, 128), F32)], axis=0)

    def t_copy(k, src):
        return remote(tiles.at[src], tiles.at[src], t_ssem.at[k], t_rsem.at[k], (e, lax.rem(s + k, SHARDS)))

    loop(1, SHARDS, lambda k: t_copy(k, s).start())
    loop(1, SHARDS, lambda k: t_copy(k, lax.rem(s + SHARDS - k, SHARDS)).wait_recv())

    every = tiles[...]
    scales = every[:, 6:7, :]
    top = jnp.max(scales, axis=0, keepdims=True)
    ratio = jnp.broadcast_to(scales / top, every.shape)
    which = lax.broadcasted_iota(jnp.int32, every.shape, 1)
    power = ratio
    weight = jnp.where(which == 0, power, 0.0)
    for k in range(1, 6):
        power = power * ratio
        weight = jnp.where(which == k, power, weight)
    moments = jnp.sum(jnp.sum(every * weight, axis=0), axis=1, keepdims=True)
    m = [None] + [moments[k:k + 1] for k in range(6)]
    top = top[0, :, 0:1]
    coef = step_scalars(m, EPS / top, EPS / top / top)
    rel = scale / top
    coef = [coef[0], coef[1] * rel, coef[2] * rel * rel]
    total = coef[0] * r0 + coef[1] * v1 + coef[2] * v2
    sg[p, c] = (FACTOR / top * total).astype(BF16)

    def s_copy(k, q):
        return remote(sg.at[q, c], sg.at[q, c], s_ssem.at[k], s_rsem.at[k], (e, 2 * chip(k) + c))

    def sf_copy(k, q):
        return remote(sg.at[q, c], sg.at[q, c], sf_ssem.at[k], sf_rsem.at[k], sib)

    def sf_wait(k, q):
        remote(sg.at[q, 1 - c], sg.at[q, 1 - c], sf_ssem.at[k], sf_rsem.at[k], sib).wait_recv()

    loop(1, CHIPS, lambda k: s_copy(k, p).start())
    sf_copy(0, p).start()

    last = r0 - rel * (coef[0] * v1 + coef[1] * v2 + coef[2] * v3)

    def add_av(k, carry):
        q = from_chip(k)
        remote(stage.at[p, 2], av.at[q], av_ssem.at[k], av_rsem.at[k], (e, 2 * q + c)).wait_recv()
        return carry + av[q].astype(F32)

    whole = lax.fori_loop(1, CHIPS, add_av, stage[p, 2].astype(F32))
    fit[...] = (whole - last).astype(BF16)
    returns = []
    for at, d in enumerate(ORDER):
        if d:
            back_copy = remote(fit.at[pl.ds(at * CAP, CAP)], ret.at[pl.ds(d * CAP, CAP)], r_ssem.at[d], r_rsem.at[d], (back(d), s))
            back_copy.start()
            returns.append(back_copy)
        else:
            ret[0:CAP] = fit[at * CAP:(at + 1) * CAP]

    def refit(q, core):
        j = 2 * q + core
        cols = pl.ds(pl.multiple_of(j * 128, 128), 128)
        w = dot(ht[...], sg[q, core]) + down[:, cols].astype(F32)
        w = jnp.concatenate([w[:128] * kb[0, pl.ds(j, 1), :], w[128:] * kb[1, pl.ds(j, 1), :]], axis=0)
        new_ref[0, :, cols] = w.astype(BF16)

    refit(p, c)

    def refit_step(k):
        q = from_chip(k)
        s_copy(k, q).wait_recv()
        sf_copy(k, q).start()
        refit(q, c)
        before = from_chip(k - 1)
        sf_wait(k - 1, before)
        refit(before, 1 - c)

    loop(1, CHIPS, refit_step)
    sf_wait(CHIPS - 1, from_chip(CHIPS - 1))
    refit(from_chip(CHIPS - 1), 1 - c)

    for back_copy in returns:
        back_copy.wait()
    refit_ref[...] = jnp.dot(combining, ret[...].astype(F32), preferred_element_type=F32,
                             precision=lax.Precision.HIGHEST).astype(BF16)

    @pl.when(c == 0)
    def _():
        z_copy(0).wait_send()

    loop(1, 4, lambda i: z_copy(i).wait_send())
    loop(0, CHIPS, lambda q: v_copy(q).wait_send())

    def drain(k):
        ag_copy(k, p).wait_send()
        rs_copy(k, chip(k)).wait_send()
        av_copy(k, chip(k)).wait_send()
        s_copy(k, p).wait_send()

    loop(1, CHIPS, drain)

    def drain_sibling(k):
        fw_copy(k, from_chip(k)).wait_send()
        sf_copy(k, from_chip(k)).wait_send()

    loop(0, CHIPS, drain_sibling)
    loop(1, SHARDS, lambda k: t_copy(k, s).wait_send())


def body(tokens, routes, router_logits, gate_weight, up_weight, down_weight, kept_blocks):
    rows, model = tokens.shape
    width = model // CHIPS
    own = gate_weight.shape[2]
    dma = pltpu.SemaphoreType.DMA
    vmem = pl.BlockSpec(memory_space=pltpu.VMEM)
    anywhere = pl.BlockSpec(memory_space=pl.ANY)
    return pl.pallas_call(
        kernel,
        out_shape=(jax.ShapeDtypeStruct((rows, DW // SHARDS), BF16), jax.ShapeDtypeStruct(down_weight.shape, BF16)),
        in_specs=[anywhere, vmem, vmem, anywhere, anywhere, anywhere, vmem],
        out_specs=(vmem, vmem),
        scratch_shapes=[
            pltpu.VMEM((rows, width), BF16),
            pltpu.VMEM((model, own), BF16),
            pltpu.VMEM((model, own), BF16),
            pltpu.VMEM((own, DW), BF16),
            pltpu.VMEM((ROWS, width), BF16),
            pltpu.VMEM((CHIPS, 2, ROWS // 2, width), BF16),
            pltpu.VMEM((ROWS, own), F32),
            pltpu.VMEM((ROWS, own), F32),
            pltpu.VMEM((ROWS, own), BF16),
            pltpu.VMEM((ROWS, own), BF16),
            pltpu.VMEM((own, ROWS), BF16),
            pltpu.VMEM((CHIPS, own, 128), BF16),
            pltpu.VMEM((2, SHARDS, 128), F32),
            pltpu.VMEM((2, SHARDS, 128), F32),
            pltpu.VMEM((4, 128, 128), F32),
            pltpu.VMEM((CHIPS, 3, 128, 128), BF16),
            pltpu.VMEM((CHIPS, 2, 128, 128), BF16),
            pltpu.VMEM((CHIPS, 128, 128), BF16),
            pltpu.VMEM((SHARDS, 8, 128), F32),
            pltpu.VMEM((CHIPS, 2, 128, 128), BF16),
            pltpu.VMEM((ROWS, 128), BF16),
            pltpu.VMEM((ROWS, 128), BF16),
            dma((4,)),
            dma((4,)), dma((4,)),
            dma((CHIPS,)), dma((CHIPS,)),
            dma((CHIPS,)), dma((CHIPS,)),
            dma((CHIPS,)), dma((CHIPS,)),
            dma((2,)), dma((2,)),
            dma((CHIPS,)), dma((CHIPS,)),
            dma((CHIPS,)), dma((CHIPS,)),
            dma((SHARDS,)), dma((SHARDS,)),
            dma((CHIPS,)), dma((CHIPS,)),
            dma((CHIPS,)), dma((CHIPS,)),
            dma((GROUPS,)), dma((GROUPS,)),
        ],
        compiler_params=pltpu.CompilerParams(collective_id=0, has_side_effects=True, vmem_limit_bytes=48 << 20),
        name="refit",
    )(tokens, routes, router_logits, gate_weight, up_weight, down_weight, kept_blocks)


def solution(mesh):
    in_specs = (
        P("expert", None),
        P("expert", None),
        P("expert", None),
        P("expert", None, "shard"),
        P("expert", None, "shard"),
        P("expert", "shard", None),
        P("expert", "shard", None),
    )
    out_specs = (P("expert", "shard"), P("expert", "shard", None))
    return jax.shard_map(body, mesh=mesh, in_specs=in_specs, out_specs=out_specs, check_vma=False)
```

time: 1050 us -> 85.1 us (0.08)
  waiting for transfers between devices: 589 us -> 0 us
  blocking collectives: 334 us -> 0 us
  Pallas kernels: 0 us -> 77.5 us
  matrix products: 55 us -> 0 us
  between operations: 20.8 us -> 0.64 us
  local copies, waits for them, and re-layouts: 22.3 us -> 6.7 us
  other arithmetic: 15 us -> 0 us
    unnamed x13 -> x0, waiting for transfers between devices: 410 us -> none
    psum x5 -> x0, blocking collectives: 321 us -> none  [the longest x3 191 us: squared_total(): return lax.psum(jnp.sum(operand * operand), 'shard')]
    all_gather x3 -> x0, waiting for transfers between devices: 140 us -> none  [adjoint(): lax.all_gather(shortened(operand), 'shard', axis=1, tiled=True)]
    pallas_call x0 -> x1, Pallas kernels: none -> 77.5 us  [body(): pl.pallas_call(kernel, out_shape=(jax.ShapeDtypeStruct((rows, DW // SHARD...]
    dot_general x12 -> x0, matrix products: 55 us -> none  [the longest x5 25.2 us: forward(): terms = factor * jnp.dot(hidden, operand, precision=highest)]
    all_to_all x1 -> x0, waiting for transfers between devices: 38.3 us -> none  [body(): lax.all_to_all(outgoing.reshape(experts, capacity, tokens.shape[1]), 'exp...]
    unnamed x25 -> x10, local copies, waits for them, and re-layouts: 21.4 us -> 6.7 us
    all_to_all x1 -> x0, blocking collectives: 13.4 us -> none  [body(): lax.all_to_all(fitted.reshape(experts, capacity, fitted.shape[1]), 'exper...]
  transfers between devices with their start and end apart: 9 -> 0, of which waited for: 9 -> 0; matrix products, arithmetic and copies ran while one was open for 0% -> 0% of each run, Pallas kernels for 0% -> 0%
where the time goes in v1:
time: 85.1 us; the launch traced here: 84.9 us
  Pallas kernels  77.5 us (91%)
  local copies, waits for them, and re-layouts  6.7 us (8%)
    pallas_call x1, Pallas kernels, body(): pl.pallas_call(kernel, out_shape=(jax.ShapeDtypeStruct((rows, DW // SHARD...  77.5 us
    unnamed x10, local copies, waits for them, and re-layouts  6.7 us

profile of v1, /device:TPU:1, one launch (start us, length us, event | category | flops | bytes accessed | tf_op | source)
XLA Modules:
  0.0 84.9 jit_solution(11660004958741862872)
XLA Ops:
  0.6 0.8 copy.9.routes_ref
  1.4 0.8 copy.10.logits_ref
  2.1 0.0 copy-start
  2.2 1.6 %copy-done = bf16[1,256,4096]{2,1,0:T(8,128)(2,1)S(1)} copy-done((bf16[1,256,4096]{2,1,0:T(8,128)(2,1)S(1)}, bf16[1,256,4096]{2,1,0:T(8,128)(2,1)}, u32[]{:S(2)}) %copy-start) | copy-done | bytes 2097176
  3.7 0.0 copy-start.1
  3.7 1.0 %copy-done.1 = bf16[32,6144]{1,0:T(8,128)(2,1)S(1)} copy-done((bf16[32,6144]{1,0:T(8,128)(2,1)S(1)}, bf16[32,6144]{1,0:T(8,128)(2,1)}, u32[]{:S(2)}) %copy-start.1) | copy-done | bytes 393240
  4.7 0.0 copy-start.2
  4.7 0.7 copy-done.2
  5.4 77.5 %refit.1 = (bf16[32,128]{1,0:T(8,128)(2,1)S(1)}, bf16[1,256,4096]{2,1,0:T(8,128)(2,1)S(1)}) custom-call(bf16[32,6144]{1,0:T(8,128)(2,1)S(1)} %copy-done.1, s32[32,2]{1,0:T(8,128)S(1)} %copy.9.routes_ref, f32[32,2]{1,0:T(8,128)S(1)} %copy.10.logits_ref, bf16[1,6144,256]{2,1,0:T(8,128)(2,1)} %gate_hbm.1, bf16[1,6144,256]{2,1,0:T(8,128)(2,1)} %up_hbm.1, ...), custom_call_target="tpu_custom_call" | custom-call | tf_op jit(solution)/shard_map/refit/pallas_call | solution.py:384
  82.9 0.6 copy.13
  83.5 1.3 %copy.14 = bf16[1,256,4096]{2,1,0:T(8,128)(2,1)} copy(bf16[1,256,4096]{2,1,0:T(8,128)(2,1)S(1)} %get-tuple-element.5) | data formatting | bytes 4194304
Async XLA Ops:
  2.1 1.6 %copy-start = (bf16[1,256,4096]{2,1,0:T(8,128)(2,1)S(1)}, bf16[1,256,4096]{2,1,0:T(8,128)(2,1)}, u32[]{:S(2)}) copy-start(bf16[1,256,4096]{2,1,0:T(8,128)(2,1)} %down_hbm.1) | copy-start | bytes 6291460
  3.7 1.0 %copy-start.1 = (bf16[32,6144]{1,0:T(8,128)(2,1)S(1)}, bf16[32,6144]{1,0:T(8,128)(2,1)}, u32[]{:S(2)}) copy-start(bf16[32,6144]{1,0:T(8,128)(2,1)} %tok_hbm.1) | copy-start | bytes 1179652
  4.7 0.7 copy-start.2

commit v2 on v1

v2 whole, which is shorter than its diff:
```python
import functools

import jax
import jax.numpy as jnp
from jax import lax
from jax.experimental import pallas as pl
from jax.experimental.pallas import tpu as pltpu
from jax.sharding import PartitionSpec as P

FF = 8192
DW = 4096
EPS = 1e-6
FACTOR = FF ** -0.5
CAP = 16
GROUPS = 8
CHIPS = 16
SHARDS = 32
ROWS = GROUPS * CAP
PACKED = 96
TINY = 1e-30
MESH = pl.DeviceIdType.MESH
F32 = jnp.float32
BF16 = jnp.bfloat16

ORDER = (1, 3, 5, 7, 0, 2, 4, 6)


def dot(a, b, ca=1, cb=0):
    return lax.dot_general(a, b, (((ca,), (cb,)), ((), ())), preferred_element_type=F32)


def slot_rows(routes, plane):
    rel = [lax.rem(routes[k:k + 1] - plane + GROUPS, GROUPS) for k in range(2)]
    tok = rel[0].shape[1]
    experts = lax.broadcasted_iota(jnp.int32, (GROUPS, tok), 0)
    onehot = [(r == experts).astype(F32) for r in rel]
    earlier = lax.broadcasted_iota(jnp.int32, (tok, tok), 0) < lax.broadcasted_iota(jnp.int32, (tok, tok), 1)
    before = dot((onehot[0] + onehot[1]).astype(BF16), earlier.astype(BF16))
    slots = [jnp.sum(before * o, axis=0, keepdims=True) for o in onehot]
    rows = lax.broadcasted_iota(jnp.int32, (ROWS, tok), 0).astype(F32)
    return [(r * CAP).astype(F32) + s == rows for r, s in zip(rel, slots)]


def packed(m):
    return jnp.concatenate([m[:64], jnp.concatenate([m[64:96, 64:], m[96:, 64:]], axis=1)], axis=0)


def unpacked(m):
    corner = jnp.concatenate([m[64:, :64], m[64:, 64:]], axis=0)
    return jnp.concatenate([m[:64], jnp.concatenate([jnp.transpose(m[:64])[64:], corner], axis=1)], axis=0)


def step_scalars(m, eps1, eps2):
    def form(p, shift):
        total = None
        size = None
        for i, a in enumerate(p):
            for j, b in enumerate(p):
                term = a * b * m[i + j + shift]
                total = term if total is None else total + term
                size = jnp.abs(term) if size is None else size + jnp.abs(term)
        return jnp.maximum(total, 0.0), size

    one = jnp.ones_like(m[1])
    r, s = [one], [one]
    gnorm, _ = form(r, 1)
    out = None
    for it in range(3):
        image, size = form(s, 2)
        image = jnp.maximum(image, 1e-6 * size)
        step = gnorm / (image + eps2)
        term = [step * a for a in s]
        out = term if out is None else [a + b for a, b in zip(out + [0.0] * (len(term) - len(out)), term)]
        if it < 2:
            r = [a - b for a, b in zip(r + [0.0], [0.0] + term)]
            fresh, _ = form(r, 1)
            beta = fresh / (gnorm + eps1)
            s = [a + b for a, b in zip(r, [beta * c for c in s] + [0.0])]
            gnorm = fresh
    return out


def kernel(tok_hbm, routes_hbm, logits_hbm, gate_hbm, up_hbm, down_hbm, kept_hbm,
           sg, ht, refit_ref,
           tok, routes, logits, kept, gate, up, down, outgoing, xg, acc_g, acc_u, hown, hsib, vsib, kb, ksib, gram,
           stage, rs, av, tiles, mine, fit, ret,
           load_sem, z_ssem, z_rsem, ag_ssem, ag_rsem, fw_ssem, fw_rsem, v_ssem, v_rsem, k_sem, h_sem,
           rs_ssem, rs_rsem, av_ssem, av_rsem, t_ssem, t_rsem, s_ssem, s_rsem, sf_ssem, sf_rsem, r_ssem, r_rsem, own_sem):
    e = lax.axis_index("expert")
    s = lax.axis_index("shard")
    p = s // 2
    c = lax.rem(s, 2)
    sib = (e, 2 * p + 1 - c)
    width = tok.shape[1]

    def offset(k):
        j = lax.rem(7 * k, CHIPS)
        return j // 4, lax.rem(j, 4)

    def chip(k):
        dy, dx = offset(k)
        return 4 * lax.rem(p // 4 + dy, 4) + lax.rem(lax.rem(p, 4) + dx, 4)

    def from_chip(k):
        dy, dx = offset(k)
        return 4 * lax.rem(p // 4 + 4 - dy, 4) + lax.rem(lax.rem(p, 4) + 4 - dx, 4)

    def plane(d):
        return lax.rem(e + d, GROUPS)

    def back(d):
        return lax.rem(e + GROUPS - d, GROUPS)

    def remote(src, dst, ssem, rsem, device):
        return pltpu.make_async_remote_copy(src_ref=src, dst_ref=dst, send_sem=ssem, recv_sem=rsem,
                                            device_id=device, device_id_type=MESH)

    def loop(lo, hi, f):
        lax.fori_loop(lo, hi, lambda k, _: (f(k), 0)[1], 0)

    pending = {}

    def finish():
        for name in list(pending):
            pending.pop(name)()

    barrier = pltpu.get_barrier_semaphore()
    loop(1, GROUPS, lambda d: pl.semaphore_signal(barrier, inc=1, device_id=(plane(d), s), device_id_type=MESH))
    loop(1, SHARDS, lambda k: pl.semaphore_signal(barrier, inc=1, device_id=(e, lax.rem(s + k, SHARDS)), device_id_type=MESH))

    loads = [
        pltpu.make_async_copy(tok_hbm.at[:, pl.ds(pl.multiple_of(p * width, 128), width)], tok, load_sem.at[0]),
        pltpu.make_async_copy(routes_hbm, routes, load_sem.at[1]),
        pltpu.make_async_copy(logits_hbm, logits, load_sem.at[2]),
        pltpu.make_async_copy(kept_hbm, kept, load_sem.at[3]),
        pltpu.make_async_copy(gate_hbm.at[0], gate, load_sem.at[4]),
        pltpu.make_async_copy(up_hbm.at[0], up, load_sem.at[5]),
        pltpu.make_async_copy(down_hbm.at[0], down, load_sem.at[6]),
    ]
    for load in loads:
        load.start()

    for load in loads[:4]:
        load.wait()
    match = slot_rows(routes[...], e)
    placing = (match[0] | match[1]).astype(BF16)
    outgoing[...] = dot(placing, tok[...]).astype(BF16)
    logit = logits[0:1] - logits[1:2]
    share = 1.0 / (1.0 + jnp.exp(-logit))
    combining = jnp.where(match[0], share, 0.0) + jnp.where(match[1], 1.0 - share, 0.0)
    row = lax.broadcasted_iota(jnp.int32, (2, 128), 0)
    for f in range(2):
        kb[f] = dot(kept[0].astype(F32), (row == f).astype(F32), 0, 0)

    pending["loads"] = lambda: [load.wait() for load in loads[4:]]
    pl.semaphore_wait(barrier, GROUPS - 1 + SHARDS - 1)

    def z_copy(i):
        d = 2 * i + 1 - c
        return remote(outgoing.at[pl.ds(pl.multiple_of(d * CAP, CAP), CAP)],
                      xg.at[p, c, pl.ds(pl.multiple_of(i * CAP, CAP), CAP)],
                      z_ssem.at[i], z_rsem.at[i], (plane(d), s))

    @pl.when(c == 0)
    def _():
        z_copy(0).start()

    @pl.when(c == 1)
    def _():
        xg[p, 1, 0:CAP] = outgoing[0:CAP]

    loop(1, 4, lambda i: z_copy(i).start())

    def z_sent():
        @pl.when(c == 0)
        def _():
            z_copy(0).wait_send()

        loop(1, 4, lambda i: z_copy(i).wait_send())

    def z_arrived():
        @pl.when(c == 0)
        def _():
            z_copy(0).wait_recv()

        loop(1, 4, lambda i: z_copy(i).wait_recv())

    pending["z"] = z_sent

    def v_copy(q):
        return remote(down_hbm.at[0, :, pl.ds(pl.multiple_of((2 * q + 1 - c) * 128, 128), 128)], vsib.at[q],
                      v_ssem.at[q], v_rsem.at[q], sib)

    loop(0, CHIPS, lambda q: v_copy(q).start())
    k_copy = remote(kb, ksib, k_sem.at[0], k_sem.at[1], sib)
    k_copy.start()
    pending["v"] = lambda: loop(0, CHIPS, lambda q: v_copy(q).wait())
    pending["k"] = k_copy.wait
    z_arrived()

    def ag_copy(k, q):
        return remote(xg.at[q, c], xg.at[q, c], ag_ssem.at[k], ag_rsem.at[k], (e, 2 * chip(k) + c))

    def fw_copy(k, q):
        return remote(xg.at[q, c], xg.at[q, c], fw_ssem.at[k], fw_rsem.at[k], sib)

    def fw_wait(k, q):
        remote(xg.at[q, 1 - c], xg.at[q, 1 - c], fw_ssem.at[k], fw_rsem.at[k], sib).wait_recv()

    loop(1, CHIPS, lambda k: ag_copy(k, p).start())
    fw_copy(0, p).start()
    pending["ag"] = lambda: loop(1, CHIPS, lambda k: ag_copy(k, p).wait_send())
    pending["fw"] = lambda: loop(0, CHIPS, lambda k: fw_copy(k, from_chip(k)).wait_send())
    pending.pop("loads")()
    acc_g[...] = jnp.zeros_like(acc_g)
    acc_u[...] = jnp.zeros_like(acc_u)

    def expand(k):
        q = from_chip(k)
        fw_wait(k, q)
        x = xg[q].reshape(ROWS, width)
        rows = pl.ds(pl.multiple_of(q * width, 128), width)
        acc_g[...] += dot(x, gate[rows, :])
        acc_u[...] += dot(x, up[rows, :])

    def gather_step(k):
        q = from_chip(k)
        ag_copy(k, q).wait_recv()
        fw_copy(k, q).start()
        expand(k - 1)

    loop(1, CHIPS, gather_step)
    expand(CHIPS - 1)
    g = acc_g[...]
    h32 = g / (1.0 + jnp.exp(-g)) * acc_u[...]
    hown[...] = h32.astype(BF16)
    h_copy = remote(hown, hsib, h_sem.at[0], h_sem.at[1], sib)
    h_copy.start()
    ht[...] = jnp.transpose(hown[...].astype(F32)).astype(BF16)

    def grams(h, base):
        for f in range(2):
            hf = h[:, f * 128:(f + 1) * 128]
            gram[base + f] = packed(FACTOR * FACTOR * dot(hf, hf, 1, 1))

    grams(hown[...], 0)
    pending.pop("v")()
    pending.pop("k")()
    h_copy.wait()
    grams(hsib[...], 2)

    def masked(v, k0, k1):
        return jnp.concatenate([v[:128] * (1.0 - k0).astype(BF16), v[128:] * (1.0 - k1).astype(BF16)], axis=0)

    def rs_copy(k, q):
        return remote(stage.at[q, pl.ds(0, PACKED + 128)], rs.at[p], rs_ssem.at[k], rs_rsem.at[k], (e, 2 * q + c))

    def av_copy(k, q):
        return remote(stage.at[q, pl.ds(PACKED + 128, 128)], av.at[p], av_ssem.at[k], av_rsem.at[k], (e, 2 * q + c))

    def partial(q):
        j = 2 * q + c
        ko = [kb[f, pl.ds(j, 1), :] for f in range(2)]
        ks = [ksib[f, pl.ds(j, 1), :] for f in range(2)]
        stage[q, 0:PACKED] = (ko[0] * gram[0] + ko[1] * gram[1] + ks[0] * gram[2] + ks[1] * gram[3]).astype(BF16)
        vo = down[:, pl.ds(pl.multiple_of(j * 128, 128), 128)]
        vs = vsib[q]
        both = dot(hown[...], jnp.concatenate([masked(vo, *ko), vo], axis=1))
        both += dot(hsib[...], jnp.concatenate([masked(vs, *ks), vs], axis=1))
        both = (FACTOR * both).astype(BF16)
        stage[q, PACKED:PACKED + 128] = both[:, :128]
        stage[q, PACKED + 128:] = both[:, 128:]

    def send_partial(k):
        q = chip(k)
        partial(q)
        rs_copy(k, q).start()

    loop(1, CHIPS, send_partial)
    pending["rs"] = lambda: loop(1, CHIPS, lambda k: rs_copy(k, chip(k)).wait_send())
    partial(p)

    def rs_in(k, q):
        return remote(stage.at[p, pl.ds(0, PACKED + 128)], rs.at[q], rs_ssem.at[k], rs_rsem.at[k], (e, 2 * q + c))

    def av_in(k, q):
        return remote(stage.at[p, pl.ds(PACKED + 128, 128)], av.at[q], av_ssem.at[k], av_rsem.at[k], (e, 2 * q + c))


    def add_up(k, carry):
        q = from_chip(k)
        rs_in(k, q).wait_recv()
        return carry + rs[q].astype(F32)

    summed = lax.fori_loop(1, CHIPS, add_up, stage[p, 0:PACKED + 128].astype(F32))
    big, r0 = unpacked(summed[:PACKED]), summed[PACKED:]

    eye = lax.broadcasted_iota(jnp.int32, (128, 128), 0) == lax.broadcasted_iota(jnp.int32, (128, 128), 1)
    scale = jnp.sum(jnp.sum(jnp.where(eye, big, 0.0), axis=0, keepdims=True), axis=1, keepdims=True)
    scale = jnp.maximum(scale, TINY)
    mb = (big / scale).astype(BF16)

    def apply(v):
        hi = v.astype(BF16)
        lo = (v - hi.astype(F32)).astype(BF16)
        w = dot(mb, jnp.concatenate([hi, lo], axis=1))
        return w[:, :128] + w[:, 128:]

    v1 = apply(r0)
    v2 = apply(v1)
    v3 = apply(v2)

    def inner(a, b):
        return jnp.sum(a * b, axis=0, keepdims=True)

    tiles[s] = jnp.concatenate(
        [inner(r0, v1), inner(v1, v1), inner(v1, v2), inner(v2, v2), inner(v2, v3), inner(v3, v3),
         jnp.broadcast_to(scale, (1, 128)), jnp.zeros((1, 128), F32)], axis=0)

    def t_copy(k, src):
        return remote(tiles.at[src], tiles.at[src], t_ssem.at[k], t_rsem.at[k], (e, lax.rem(s + k, SHARDS)))

    loop(1, SHARDS, lambda k: t_copy(k, s).start())
    loop(1, CHIPS, lambda k: av_copy(k, chip(k)).start())
    pending["av"] = lambda: loop(1, CHIPS, lambda k: av_copy(k, chip(k)).wait_send())
    pending["av in"] = lambda: loop(1, CHIPS, lambda k: av_in(k, from_chip(k)).wait_recv())
    pending["t"] = lambda: loop(1, SHARDS, lambda k: t_copy(k, s).wait_send())
    loop(1, SHARDS, lambda k: t_copy(k, lax.rem(s + SHARDS - k, SHARDS)).wait_recv())

    every = tiles[...]
    scales = every[:, 6:7, :]
    top = jnp.max(scales, axis=0, keepdims=True)
    ratio = jnp.broadcast_to(scales / top, every.shape)
    which = lax.broadcasted_iota(jnp.int32, every.shape, 1)
    power = ratio
    weight = jnp.where(which == 0, power, 0.0)
    for k in range(1, 6):
        power = power * ratio
        weight = jnp.where(which == k, power, weight)
    moments = jnp.sum(jnp.sum(every * weight, axis=0), axis=1, keepdims=True)
    m = [None] + [moments[k:k + 1] for k in range(6)]
    top = top[0, :, 0:1]
    coef = step_scalars(m, EPS / top, EPS / top / top)
    rel = scale / top
    coef = [coef[0], coef[1] * rel, coef[2] * rel * rel]
    total = coef[0] * r0 + coef[1] * v1 + coef[2] * v2
    mine[...] = (FACTOR / top * total).astype(BF16)

    own_copy = pltpu.make_async_copy(mine, sg.at[p, c], own_sem)
    own_copy.start()

    def s_copy(k):
        return remote(mine, sg.at[p, c], s_ssem.at[k], s_rsem.at[k], (e, 2 * chip(k) + c))

    def s_in(k, q):
        return remote(mine, sg.at[q, c], s_ssem.at[k], s_rsem.at[k], (e, 2 * chip(k) + c))

    def sf_copy(k, q):
        return remote(sg.at[q, c], sg.at[q, c], sf_ssem.at[k], sf_rsem.at[k], sib)

    def sf_wait(k, q):
        remote(sg.at[q, 1 - c], sg.at[q, 1 - c], sf_ssem.at[k], sf_rsem.at[k], sib).wait_recv()

    own_share = remote(mine, sg.at[p, c], sf_ssem.at[0], sf_rsem.at[0], sib)
    own_share.start()
    loop(1, CHIPS, lambda k: s_copy(k).start())
    pending["s"] = lambda: loop(1, CHIPS, lambda k: s_copy(k).wait_send())
    pending["sf"] = lambda: (own_share.wait_send(), loop(1, CHIPS, lambda k: sf_copy(k, from_chip(k)).wait_send()))
    pending["own"] = own_copy.wait

    last = r0 - rel * (coef[0] * v1 + coef[1] * v2 + coef[2] * v3)

    def add_av(k, carry):
        q = from_chip(k)
        av_in(k, q).wait_recv()
        return carry + av[q].astype(F32)

    pending.pop("av in")
    whole = lax.fori_loop(1, CHIPS, add_av, stage[p, PACKED + 128:].astype(F32))
    fit[...] = (whole - last).astype(BF16)
    returns = []
    for at, d in enumerate(ORDER):
        if d:
            back_copy = remote(fit.at[pl.ds(at * CAP, CAP)], ret.at[pl.ds(d * CAP, CAP)], r_ssem.at[d], r_rsem.at[d], (back(d), s))
            back_copy.start()
            returns.append(back_copy)
        else:
            ret[0:CAP] = fit[at * CAP:(at + 1) * CAP]

    def share_step(k):
        q = from_chip(k)
        s_in(k, q).wait_recv()
        sf_copy(k, q).start()

    loop(1, CHIPS, share_step)

    for back_copy in returns:
        back_copy.wait()
    refit_ref[...] = lax.dot_general(combining, ret[...].astype(F32), (((0,), (0,)), ((), ())),
                                     precision=lax.Precision.HIGHEST, preferred_element_type=F32).astype(BF16)
    loop(0, CHIPS, lambda k: sf_wait(k, from_chip(k)))
    finish()


PIECES = 4


def apply_kernel(sg_hbm, ht_hbm, refit_hbm, down_hbm, kept_hbm, refit_ref, new_hbm, sg, ht, down, kept, new, sem, out_sem):
    wide = DW // PIECES
    chips = CHIPS // PIECES

    def cols(i):
        return pl.ds(i * wide, wide)

    small = [pltpu.make_async_copy(a, b, sem.at[i]) for i, (a, b) in enumerate([(ht_hbm, ht), (kept_hbm, kept), (refit_hbm, refit_ref)])]
    parts = []
    for i in range(PIECES):
        parts.append((
            pltpu.make_async_copy(sg_hbm.at[pl.ds(i * chips, chips)], sg.at[pl.ds(i * chips, chips)], sem.at[3 + 2 * i]),
            pltpu.make_async_copy(down_hbm.at[0, :, cols(i)], down.at[:, cols(i)], sem.at[4 + 2 * i])))
    for copy in small[:2] + [copy for part in parts for copy in part] + small[2:]:
        copy.start()
    small[0].wait()
    small[1].wait()
    h = ht[...]
    row = lax.broadcasted_iota(jnp.int32, (2, 128), 0)
    keeps = [dot(kept[0].astype(F32), (row == f).astype(F32), 0, 0) for f in range(2)]
    writes = []
    for i in range(PIECES):
        for copy in parts[i]:
            copy.wait()
        for n in range(2 * chips):
            j = 2 * chips * i + n
            at = slice(j * 128, (j + 1) * 128)
            w = dot(h, sg[j // 2, j % 2]) + down[:, at].astype(F32)
            new[:128, at] = (w[:128] * keeps[0][j:j + 1]).astype(BF16)
            new[128:, at] = (w[128:] * keeps[1][j:j + 1]).astype(BF16)
        write = pltpu.make_async_copy(new.at[:, cols(i)], new_hbm.at[0, :, cols(i)], out_sem.at[i])
        write.start()
        writes.append(write)
    for copy in writes + small[2:]:
        copy.wait()


def body(tokens, routes, router_logits, gate_weight, up_weight, down_weight, kept_blocks):
    rows, model = tokens.shape
    width = model // CHIPS
    own = gate_weight.shape[2]
    dma = pltpu.SemaphoreType.DMA
    vmem = pl.BlockSpec(memory_space=pltpu.VMEM)
    hbm = pl.BlockSpec(memory_space=pltpu.HBM)
    gathered, turned, refit = pl.pallas_call(
        kernel,
        out_shape=(jax.ShapeDtypeStruct((CHIPS, 2, 128, 128), BF16), jax.ShapeDtypeStruct((own, ROWS), BF16),
                   jax.ShapeDtypeStruct((rows, DW // SHARDS), BF16)),
        in_specs=[hbm] * 7,
        out_specs=(hbm, vmem, vmem),
        scratch_shapes=[
            pltpu.VMEM((rows, width), BF16),
            pltpu.VMEM((2, rows), jnp.int32),
            pltpu.VMEM((2, rows), F32),
            pltpu.VMEM(kept_blocks.shape, jnp.int32),
            pltpu.VMEM((model, own), BF16),
            pltpu.VMEM((model, own), BF16),
            pltpu.VMEM((own, DW), BF16),
            pltpu.VMEM((ROWS, width), BF16),
            pltpu.VMEM((CHIPS, 2, ROWS // 2, width), BF16),
            pltpu.VMEM((ROWS, own), F32),
            pltpu.VMEM((ROWS, own), F32),
            pltpu.VMEM((ROWS, own), BF16),
            pltpu.VMEM((ROWS, own), BF16),
            pltpu.VMEM((CHIPS, own, 128), BF16),
            pltpu.VMEM((2, SHARDS, 128), F32),
            pltpu.VMEM((2, SHARDS, 128), F32),
            pltpu.VMEM((4, PACKED, 128), F32),
            pltpu.VMEM((CHIPS, PACKED + 256, 128), BF16),
            pltpu.VMEM((CHIPS, PACKED + 128, 128), BF16),
            pltpu.VMEM((CHIPS, 128, 128), BF16),
            pltpu.VMEM((SHARDS, 8, 128), F32),
            pltpu.VMEM((ROWS, 128), BF16),
            pltpu.VMEM((ROWS, 128), BF16),
            pltpu.VMEM((ROWS, 128), BF16),
            dma((7,)),
            dma((4,)), dma((4,)),
            dma((CHIPS,)), dma((CHIPS,)),
            dma((CHIPS,)), dma((CHIPS,)),
            dma((CHIPS,)), dma((CHIPS,)),
            dma((2,)), dma((2,)),
            dma((CHIPS,)), dma((CHIPS,)),
            dma((CHIPS,)), dma((CHIPS,)),
            dma((SHARDS,)), dma((SHARDS,)),
            dma((CHIPS,)), dma((CHIPS,)),
            dma((CHIPS,)), dma((CHIPS,)),
            dma((GROUPS,)), dma((GROUPS,)),
            dma,
        ],
        compiler_params=pltpu.CompilerParams(collective_id=0, has_side_effects=True, vmem_limit_bytes=60 << 20),
        name="refit",
    )(tokens, routes.T, router_logits.T, gate_weight, up_weight, down_weight, kept_blocks)
    return pl.pallas_call(
        apply_kernel,
        out_shape=(jax.ShapeDtypeStruct(refit.shape, BF16), jax.ShapeDtypeStruct(down_weight.shape, BF16)),
        in_specs=[hbm] * 5,
        out_specs=(vmem, hbm),
        scratch_shapes=[
            pltpu.VMEM(gathered.shape, BF16),
            pltpu.VMEM(turned.shape, BF16),
            pltpu.VMEM((own, DW), BF16),
            pltpu.VMEM(kept_blocks.shape, jnp.int32),
            pltpu.VMEM((own, DW), BF16),
            dma((3 + 2 * PIECES,)),
            dma((PIECES,)),
        ],
        compiler_params=pltpu.CompilerParams(vmem_limit_bytes=60 << 20),
        name="apply",
    )(gathered, turned, refit, down_weight, kept_blocks)


def solution(mesh):
    in_specs = (
        P("expert", None),
        P("expert", None),
        P("expert", None),
        P("expert", None, "shard"),
        P("expert", None, "shard"),
        P("expert", "shard", None),
        P("expert", "shard", None),
    )
    out_specs = (P("expert", "shard"), P("expert", "shard", None))
    return jax.shard_map(body, mesh=mesh, in_specs=in_specs, out_specs=out_specs, check_vma=False)
```

time: 85.1 us -> 72.6 us (0.85)
  local copies, waits for them, and re-layouts: 6.7 us -> 0 us
  Pallas kernels: 77.5 us -> 71.9 us
    unnamed x10 -> x0, local copies, waits for them, and re-layouts: 6.7 us -> none
    pallas_call x1 -> x2, Pallas kernels: 77.5 us -> 71.9 us  [the longest x1 68 us: body(): pl.pallas_call(kernel, out_shape=(jax.ShapeDtypeStruct((CHIPS, 2, 128, 12...]
where the time goes in v2:
time: 72.6 us; the launch traced here: 72.5 us
  Pallas kernels  71.9 us (99%)
    pallas_call x1, Pallas kernels, body(): pl.pallas_call(kernel, out_shape=(jax.ShapeDtypeStruct((CHIPS, 2, 128, 12...  68 us
    pallas_call x1, Pallas kernels, body(): pl.pallas_call(apply_kernel, out_shape=(jax.ShapeDtypeStruct(refit.shape,...  3.86 us

profile of v2, /device:TPU:1, one launch (start us, length us, event | category | flops | bytes accessed | tf_op | source)
XLA Modules:
  0.0 72.5 jit_solution(15408293245583125139)
XLA Ops:
  0.6 68.0 %refit.1 = (bf16[16,2,128,128]{3,2,1,0:T(8,128)(2,1)}, bf16[256,128]{1,0:T(8,128)(2,1)}, bf16[32,128]{1,0:T(8,128)(2,1)}) custom-call(bf16[32,6144]{1,0:T(8,128)(2,1)} %tok_hbm.1, s32[2,32]{1,0:T(2,128)} %bitcast.2, f32[2,32]{1,0:T(2,128)} %bitcast.3, bf16[1,6144,256]{2,1,0:T(8,128)(2,1)} %gate_hbm.1, bf16[1,6144,256]{2,1,0:T(8,128)(2,1)} %up_hbm.1, ...), custom_call_target="tpu_custom_call" | custom-call | tf_op jit(solution)/shard_map/refit/pallas_call | solution.py:452
  68.7 3.9 %apply.1 = (bf16[32,128]{1,0:T(8,128)(2,1)}, bf16[1,256,4096]{2,1,0:T(8,128)(2,1)}) custom-call(bf16[16,2,128,128]{3,2,1,0:T(8,128)(2,1)} %get-tuple-element.5.sg_hbm, bf16[256,128]{1,0:T(8,128)(2,1)} %get-tuple-element.6.ht_hbm, bf16[32,128]{1,0:T(8,128)(2,1)} %get-tuple-element.7.refit_hbm, bf16[1,256,4096]{2,1,0:T(8,128)(2,1)} %down_hbm.3, ...), custom_call_target="tpu_custom_call" | custom-call | tf_op jit(solution)/shard_map/apply/pallas_call | solution.py:500

commit v3 on v2

--- a/solution.py
+++ b/solution.py
@@ -82,9 +82,9 @@
 
 def kernel(tok_hbm, routes_hbm, logits_hbm, gate_hbm, up_hbm, down_hbm, kept_hbm,
            sg, ht, refit_ref,
-           tok, routes, logits, kept, gate, up, down, outgoing, xg, acc_g, acc_u, hown, hsib, vsib, kb, ksib, gram,
+           tok, tokd, routes, logits, kept, gate, up, down, outgoing, outd, xg, xd, acc_g, acc_u, hown, hsib, vsib, kb, ksib, gram,
            stage, rs, av, tiles, mine, fit, ret,
-           load_sem, z_ssem, z_rsem, ag_ssem, ag_rsem, fw_ssem, fw_rsem, v_ssem, v_rsem, k_sem, h_sem,
+           load_sem, z_ssem, z_rsem, d_ssem, d_rsem, df_ssem, df_rsem, ag_ssem, ag_rsem, fw_ssem, fw_rsem, v_ssem, v_rsem, k_sem, h_sem,
            rs_ssem, rs_rsem, av_ssem, av_rsem, t_ssem, t_rsem, s_ssem, s_rsem, sf_ssem, sf_rsem, r_ssem, r_rsem, own_sem):
     e = lax.axis_index("expert")
     s = lax.axis_index("shard")
@@ -92,6 +92,8 @@
     c = lax.rem(s, 2)
     sib = (e, 2 * p + 1 - c)
     width = tok.shape[1]
+    direct = tokd.shape[1]
+    planar = CHIPS * width
 
     def offset(k):
         j = lax.rem(7 * k, CHIPS)
@@ -136,8 +138,9 @@
         pltpu.make_async_copy(gate_hbm.at[0], gate, load_sem.at[4]),
         pltpu.make_async_copy(up_hbm.at[0], up, load_sem.at[5]),
         pltpu.make_async_copy(down_hbm.at[0], down, load_sem.at[6]),
+        pltpu.make_async_copy(tok_hbm.at[:, pl.ds(planar, direct)], tokd, load_sem.at[7]),
     ]
-    for load in loads:
+    for load in [loads[0], loads[7]] + loads[1:7]:
         load.start()
 
     for load in loads[:4]:
@@ -145,6 +148,8 @@
     match = slot_rows(routes[...], e)
     placing = (match[0] | match[1]).astype(BF16)
     outgoing[...] = dot(placing, tok[...]).astype(BF16)
+    loads[7].wait()
+    outd[...] = dot(placing, tokd[...]).astype(BF16)
     logit = logits[0:1] - logits[1:2]
     share = 1.0 / (1.0 + jnp.exp(-logit))
     combining = jnp.where(match[0], share, 0.0) + jnp.where(match[1], 1.0 - share, 0.0)
@@ -152,31 +157,45 @@
     for f in range(2):
         kb[f] = dot(kept[0].astype(F32), (row == f).astype(F32), 0, 0)
 
-    pending["loads"] = lambda: [load.wait() for load in loads[4:]]
+    pending["loads"] = lambda: [load.wait() for load in loads[4:7]]
     pl.semaphore_wait(barrier, GROUPS - 1 + SHARDS - 1)
+
+    def slots(i):
+        return pl.ds(pl.multiple_of(i * CAP, CAP), CAP)
 
     def z_copy(i):
         d = 2 * i + 1 - c
-        return remote(outgoing.at[pl.ds(pl.multiple_of(d * CAP, CAP), CAP)],
-                      xg.at[p, c, pl.ds(pl.multiple_of(i * CAP, CAP), CAP)],
-                      z_ssem.at[i], z_rsem.at[i], (plane(d), s))
+        return remote(outgoing.at[slots(d)], xg.at[p, c, slots(i)], z_ssem.at[i], z_rsem.at[i], (plane(d), s))
+
+    def d_copy(i):
+        d = 2 * i + 1 - c
+        return remote(outd.at[slots(d)], xd.at[c, slots(i)], d_ssem.at[i], d_rsem.at[i], (plane(d), s))
 
     @pl.when(c == 0)
     def _():
         z_copy(0).start()
 
+    loop(1, 4, lambda i: z_copy(i).start())
+
+    @pl.when(c == 0)
+    def _():
+        d_copy(0).start()
+
+    loop(1, 4, lambda i: d_copy(i).start())
+
     @pl.when(c == 1)
     def _():
         xg[p, 1, 0:CAP] = outgoing[0:CAP]
-
-    loop(1, 4, lambda i: z_copy(i).start())
+        xd[1, 0:CAP] = outd[0:CAP]
 
     def z_sent():
         @pl.when(c == 0)
         def _():
             z_copy(0).wait_send()
+            d_copy(0).wait_send()
 
         loop(1, 4, lambda i: z_copy(i).wait_send())
+        loop(1, 4, lambda i: d_copy(i).wait_send())
 
     def z_arrived():
         @pl.when(c == 0)
@@ -210,6 +229,25 @@
     loop(1, CHIPS, lambda k: ag_copy(k, p).start())
     fw_copy(0, p).start()
     pending["ag"] = lambda: loop(1, CHIPS, lambda k: ag_copy(k, p).wait_send())
+
+    def df_copy(i):
+        return remote(xd.at[c, slots(i)], xd.at[c, slots(i)], df_ssem.at[i], df_rsem.at[i], sib)
+
+    def df_wait(i):
+        remote(xd.at[1 - c, slots(i)], xd.at[1 - c, slots(i)], df_ssem.at[i], df_rsem.at[i], sib).wait_recv()
+
+    @pl.when(c == 0)
+    def _():
+        d_copy(0).wait_recv()
+
+    df_copy(0).start()
+
+    def direct_step(i):
+        d_copy(i).wait_recv()
+        df_copy(i).start()
+
+    loop(1, 4, direct_step)
+    pending["df"] = lambda: loop(0, 4, lambda i: df_copy(i).wait_send())
     pending["fw"] = lambda: loop(0, CHIPS, lambda k: fw_copy(k, from_chip(k)).wait_send())
     pending.pop("loads")()
     acc_g[...] = jnp.zeros_like(acc_g)
@@ -223,14 +261,34 @@
         acc_g[...] += dot(x, gate[rows, :])
         acc_u[...] += dot(x, up[rows, :])
 
+    def expand_direct(n):
+        x = xd[:, :, pl.ds(pl.multiple_of(n * width, 128), width)].reshape(ROWS, width)
+        rows = pl.ds(pl.multiple_of(planar + n * width, 128), width)
+        acc_g[...] += dot(x, gate[rows, :])
+        acc_u[...] += dot(x, up[rows, :])
+
     def gather_step(k):
         q = from_chip(k)
         ag_copy(k, q).wait_recv()
         fw_copy(k, q).start()
-        expand(k - 1)
-
-    loop(1, CHIPS, gather_step)
-    expand(CHIPS - 1)
+
+    half = direct // width
+    gather_step(1)
+    loop(0, 4, df_wait)
+    expand_direct(0)
+
+    def early(k):
+        gather_step(k)
+        expand_direct(k - 1)
+
+    def late(k):
+        gather_step(k)
+        expand(2 * (k - half - 1))
+        expand(2 * (k - half - 1) + 1)
+
+    loop(2, half + 1, early)
+    loop(half + 1, CHIPS, late)
+    loop(2 * (CHIPS - half - 1), CHIPS, expand)
     g = acc_g[...]
     h32 = g / (1.0 + jnp.exp(-g)) * acc_u[...]
     hown[...] = h32.astype(BF16)
@@ -444,7 +502,8 @@
 
 def body(tokens, routes, router_logits, gate_weight, up_weight, down_weight, kept_blocks):
     rows, model = tokens.shape
-    width = model // CHIPS
+    width = model * 2 // (3 * CHIPS)
+    direct = model // 3
     own = gate_weight.shape[2]
     dma = pltpu.SemaphoreType.DMA
     vmem = pl.BlockSpec(memory_space=pltpu.VMEM)
@@ -457,6 +516,7 @@
         out_specs=(hbm, vmem, vmem),
         scratch_shapes=[
             pltpu.VMEM((rows, width), BF16),
+            pltpu.VMEM((rows, direct), BF16),
             pltpu.VMEM((2, rows), jnp.int32),
             pltpu.VMEM((2, rows), F32),
             pltpu.VMEM(kept_blocks.shape, jnp.int32),
@@ -464,7 +524,9 @@
             pltpu.VMEM((model, own), BF16),
             pltpu.VMEM((own, DW), BF16),
             pltpu.VMEM((ROWS, width), BF16),
+            pltpu.VMEM((ROWS, direct), BF16),
             pltpu.VMEM((CHIPS, 2, ROWS // 2, width), BF16),
+            pltpu.VMEM((2, ROWS // 2, direct), BF16),
             pltpu.VMEM((ROWS, own), F32),
             pltpu.VMEM((ROWS, own), F32),
             pltpu.VMEM((ROWS, own), BF16),
@@ -480,7 +542,9 @@
             pltpu.VMEM((ROWS, 128), BF16),
             pltpu.VMEM((ROWS, 128), BF16),
             pltpu.VMEM((ROWS, 128), BF16),
-            dma((7,)),
+            dma((8,)),
+            dma((4,)), dma((4,)),
+            dma((4,)), dma((4,)),
             dma((4,)), dma((4,)),
             dma((CHIPS,)), dma((CHIPS,)),
             dma((CHIPS,)), dma((CHIPS,)),

time: 72.6 us -> 69.2 us (0.953)
  Pallas kernels: 71.9 us -> 68.4 us
    pallas_call x1, Pallas kernels: 68 us -> 64.6 us  [body(): pl.pallas_call(kernel, out_shape=(jax.ShapeDtypeStruct((CHIPS, 2, 128, 12...]
where the time goes in v3:
time: 69.2 us; the launch traced here: 69.1 us
  Pallas kernels  68.4 us (99%)
    pallas_call x1, Pallas kernels, body(): pl.pallas_call(kernel, out_shape=(jax.ShapeDtypeStruct((CHIPS, 2, 128, 12...  64.6 us
    pallas_call x1, Pallas kernels, body(): pl.pallas_call(apply_kernel, out_shape=(jax.ShapeDtypeStruct(refit.shape,...  3.86 us

profile of v3, /device:TPU:1, one launch (start us, length us, event | category | flops | bytes accessed | tf_op | source)
XLA Modules:
  0.0 69.1 jit_solution(14385048226637755620)
XLA Ops:
  0.6 64.6 %refit.1 = (bf16[16,2,128,128]{3,2,1,0:T(8,128)(2,1)}, bf16[256,128]{1,0:T(8,128)(2,1)}, bf16[32,128]{1,0:T(8,128)(2,1)}) custom-call(bf16[32,6144]{1,0:T(8,128)(2,1)} %tok_hbm.1, s32[2,32]{1,0:T(2,128)} %bitcast.2, f32[2,32]{1,0:T(2,128)} %bitcast.3, bf16[1,6144,256]{2,1,0:T(8,128)(2,1)} %gate_hbm.1, bf16[1,6144,256]{2,1,0:T(8,128)(2,1)} %up_hbm.1, ...), custom_call_target="tpu_custom_call" | custom-call | tf_op jit(solution)/shard_map/refit/pallas_call | solution.py:511
  65.2 3.9 %apply.1 = (bf16[32,128]{1,0:T(8,128)(2,1)}, bf16[1,256,4096]{2,1,0:T(8,128)(2,1)}) custom-call(bf16[16,2,128,128]{3,2,1,0:T(8,128)(2,1)} %get-tuple-element.5.sg_hbm, bf16[256,128]{1,0:T(8,128)(2,1)} %get-tuple-element.6.ht_hbm, bf16[32,128]{1,0:T(8,128)(2,1)} %get-tuple-element.7.refit_hbm, bf16[1,256,4096]{2,1,0:T(8,128)(2,1)} %down_hbm.3, ...), custom_call_target="tpu_custom_call" | custom-call | tf_op jit(solution)/shard_map/apply/pallas_call | solution.py:564

commit v4 on v3

--- a/solution.py
+++ b/solution.py
@@ -17,6 +17,7 @@
 SHARDS = 32
 ROWS = GROUPS * CAP
 PACKED = 96
+HALF = (PACKED + 128) // 2
 TINY = 1e-30
 MESH = pl.DeviceIdType.MESH
 F32 = jnp.float32
@@ -83,9 +84,9 @@
 def kernel(tok_hbm, routes_hbm, logits_hbm, gate_hbm, up_hbm, down_hbm, kept_hbm,
            sg, ht, refit_ref,
            tok, tokd, routes, logits, kept, gate, up, down, outgoing, outd, xg, xd, acc_g, acc_u, hown, hsib, vsib, kb, ksib, gram,
-           stage, rs, av, tiles, mine, fit, ret,
+           stage, one, relay, two, av, tiles, mine, fit, ret,
            load_sem, z_ssem, z_rsem, d_ssem, d_rsem, df_ssem, df_rsem, ag_ssem, ag_rsem, fw_ssem, fw_rsem, v_ssem, v_rsem, k_sem, h_sem,
-           rs_ssem, rs_rsem, av_ssem, av_rsem, t_ssem, t_rsem, s_ssem, s_rsem, sf_ssem, sf_rsem, r_ssem, r_rsem, own_sem):
+           one_ssem, one_rsem, two_ssem, two_rsem, av_ssem, av_rsem, t_ssem, t_rsem, s_ssem, s_rsem, sf_ssem, sf_rsem, r_ssem, r_rsem, own_sem):
     e = lax.axis_index("expert")
     s = lax.axis_index("shard")
     p = s // 2
@@ -310,9 +311,6 @@
     def masked(v, k0, k1):
         return jnp.concatenate([v[:128] * (1.0 - k0).astype(BF16), v[128:] * (1.0 - k1).astype(BF16)], axis=0)
 
-    def rs_copy(k, q):
-        return remote(stage.at[q, pl.ds(0, PACKED + 128)], rs.at[p], rs_ssem.at[k], rs_rsem.at[k], (e, 2 * q + c))
-
     def av_copy(k, q):
         return remote(stage.at[q, pl.ds(PACKED + 128, 128)], av.at[p], av_ssem.at[k], av_rsem.at[k], (e, 2 * q + c))
 
@@ -329,29 +327,68 @@
         stage[q, PACKED:PACKED + 128] = both[:, :128]
         stage[q, PACKED + 128:] = both[:, 128:]
 
-    def send_partial(k):
-        q = chip(k)
-        partial(q)
-        rs_copy(k, q).start()
-
-    loop(1, CHIPS, send_partial)
-    pending["rs"] = lambda: loop(1, CHIPS, lambda k: rs_copy(k, chip(k)).wait_send())
+    def across(dy, dx):
+        return 4 * lax.rem(p // 4 + dy, 4) + lax.rem(lax.rem(p, 4) + dx, 4)
+
+    def first(way, far, step):
+        q = across(far, step) if way == 0 else across(step, far)
+        to = across(0, step) if way == 0 else across(step, 0)
+        i = 4 * (step - 1) + far
+        return remote(stage.at[q, pl.ds(way * HALF, HALF)], one.at[way, i], one_ssem.at[way, i], one_rsem.at[way, i], (e, 2 * to + c))
+
+    def second(way, far):
+        to = across(far, 0) if way == 0 else across(0, far)
+        return remote(relay.at[way, far - 1], two.at[way, far - 1], two_ssem.at[way, far - 1], two_rsem.at[way, far - 1], (e, 2 * to + c))
+
+    def send_far(n):
+        dy, dx = n // 3 + 1, lax.rem(n, 3) + 1
+        partial(across(dy, dx))
+        first(0, dy, dx).start()
+        first(1, dx, dy).start()
+
+    def send_near(d):
+        partial(across(0, d))
+        first(0, 0, d).start()
+        partial(across(d, 0))
+        first(1, 0, d).start()
+
+    loop(0, 9, send_far)
+    loop(1, 4, send_near)
     partial(p)
 
-    def rs_in(k, q):
-        return remote(stage.at[p, pl.ds(0, PACKED + 128)], rs.at[q], rs_ssem.at[k], rs_rsem.at[k], (e, 2 * q + c))
+    def firsts_sent(n):
+        far, step = lax.rem(n, 4), n // 4 + 1
+        first(0, far, step).wait_send()
+        first(1, far, step).wait_send()
+
+    pending["one"] = lambda: loop(0, 12, firsts_sent)
+
+    def gathered(way, far):
+        q = across(far, 0) if way == 0 else across(0, far)
+        total = stage[q, way * HALF:(way + 1) * HALF].astype(F32)
+        for step in range(1, 4):
+            first(way, far, step).wait_recv()
+            total += one[way, 4 * (step - 1) + far].astype(F32)
+        return total
+
+    for far in range(1, 4):
+        for way in range(2):
+            relay[way, far - 1] = gathered(way, far).astype(BF16)
+            second(way, far).start()
+
+    pending["two"] = lambda: [second(way, far).wait_send() for way in range(2) for far in range(1, 4)]
+    halves = [gathered(way, 0) for way in range(2)]
+    for far in range(1, 4):
+        for way in range(2):
+            second(way, far).wait_recv()
+            halves[way] += two[way, far - 1].astype(F32)
+
+    summed = jnp.concatenate(halves, axis=0)
+    big, r0 = unpacked(summed[:PACKED]), summed[PACKED:]
 
     def av_in(k, q):
         return remote(stage.at[p, pl.ds(PACKED + 128, 128)], av.at[q], av_ssem.at[k], av_rsem.at[k], (e, 2 * q + c))
 
-
-    def add_up(k, carry):
-        q = from_chip(k)
-        rs_in(k, q).wait_recv()
-        return carry + rs[q].astype(F32)
-
-    summed = lax.fori_loop(1, CHIPS, add_up, stage[p, 0:PACKED + 128].astype(F32))
-    big, r0 = unpacked(summed[:PACKED]), summed[PACKED:]
 
     eye = lax.broadcasted_iota(jnp.int32, (128, 128), 0) == lax.broadcasted_iota(jnp.int32, (128, 128), 1)
     scale = jnp.sum(jnp.sum(jnp.where(eye, big, 0.0), axis=0, keepdims=True), axis=1, keepdims=True)
@@ -536,7 +573,9 @@
             pltpu.VMEM((2, SHARDS, 128), F32),
             pltpu.VMEM((4, PACKED, 128), F32),
             pltpu.VMEM((CHIPS, PACKED + 256, 128), BF16),
-            pltpu.VMEM((CHIPS, PACKED + 128, 128), BF16),
+            pltpu.VMEM((2, 12, HALF, 128), BF16),
+            pltpu.VMEM((2, 3, HALF, 128), BF16),
+            pltpu.VMEM((2, 3, HALF, 128), BF16),
             pltpu.VMEM((CHIPS, 128, 128), BF16),
             pltpu.VMEM((SHARDS, 8, 128), F32),
             pltpu.VMEM((ROWS, 128), BF16),
@@ -550,7 +589,8 @@
             dma((CHIPS,)), dma((CHIPS,)),
             dma((CHIPS,)), dma((CHIPS,)),
             dma((2,)), dma((2,)),
-            dma((CHIPS,)), dma((CHIPS,)),
+            dma((2, 12)), dma((2, 12)),
+            dma((2, 3)), dma((2, 3)),
             dma((CHIPS,)), dma((CHIPS,)),
             dma((SHARDS,)), dma((SHARDS,)),
             dma((CHIPS,)), dma((CHIPS,)),

time: 69.2 us -> 66 us (0.954)
  Pallas kernels: 68.4 us -> 65.2 us
    pallas_call x1, Pallas kernels: 64.6 us -> 61.4 us  [body(): pl.pallas_call(kernel, out_shape=(jax.ShapeDtypeStruct((CHIPS, 2, 128, 12...]
where the time goes in v4:
time: 66 us; the launch traced here: 65.9 us
  Pallas kernels  65.2 us (99%)
    pallas_call x1, Pallas kernels, body(): pl.pallas_call(kernel, out_shape=(jax.ShapeDtypeStruct((CHIPS, 2, 128, 12...  61.4 us
    pallas_call x1, Pallas kernels, body(): pl.pallas_call(apply_kernel, out_shape=(jax.ShapeDtypeStruct(refit.shape,...  3.86 us

profile of v4, /device:TPU:1, one launch (start us, length us, event | category | flops | bytes accessed | tf_op | source)
XLA Modules:
  0.0 65.9 jit_solution(13780765432132548767)
XLA Ops:
  0.6 61.4 %refit.1 = (bf16[16,2,128,128]{3,2,1,0:T(8,128)(2,1)}, bf16[256,128]{1,0:T(8,128)(2,1)}, bf16[32,128]{1,0:T(8,128)(2,1)}) custom-call(bf16[32,6144]{1,0:T(8,128)(2,1)} %tok_hbm.1, s32[2,32]{1,0:T(2,128)} %bitcast.2, f32[2,32]{1,0:T(2,128)} %bitcast.3, bf16[1,6144,256]{2,1,0:T(8,128)(2,1)} %gate_hbm.1, bf16[1,6144,256]{2,1,0:T(8,128)(2,1)} %up_hbm.1, ...), custom_call_target="tpu_custom_call" | custom-call | tf_op jit(solution)/shard_map/refit/pallas_call | solution.py:548
  62.0 3.9 %apply.1 = (bf16[32,128]{1,0:T(8,128)(2,1)}, bf16[1,256,4096]{2,1,0:T(8,128)(2,1)}) custom-call(bf16[16,2,128,128]{3,2,1,0:T(8,128)(2,1)} %get-tuple-element.5.sg_hbm, bf16[256,128]{1,0:T(8,128)(2,1)} %get-tuple-element.6.ht_hbm, bf16[32,128]{1,0:T(8,128)(2,1)} %get-tuple-element.7.refit_hbm, bf16[1,256,4096]{2,1,0:T(8,128)(2,1)} %down_hbm.3, ...), custom_call_target="tpu_custom_call" | custom-call | tf_op jit(solution)/shard_map/apply/pallas_call | solution.py:604

commit v5 on v4

--- a/solution.py
+++ b/solution.py
@@ -82,11 +82,11 @@
 
 
 def kernel(tok_hbm, routes_hbm, logits_hbm, gate_hbm, up_hbm, down_hbm, kept_hbm,
-           sg, ht, refit_ref,
-           tok, tokd, routes, logits, kept, gate, up, down, outgoing, outd, xg, xd, acc_g, acc_u, hown, hsib, vsib, kb, ksib, gram,
-           stage, one, relay, two, av, tiles, mine, fit, ret,
+           sg, ht_hbm, refit_hbm,
+           tok, tokd, routes, logits, kept, gate, up, down, outgoing, outd, xg, xd, acc_g, acc_u, hown, hsib, ht, vsib, kb, ksib, gram,
+           stage, one, relay, two, av, tiles, mine, fit, ret, refitted,
            load_sem, z_ssem, z_rsem, d_ssem, d_rsem, df_ssem, df_rsem, ag_ssem, ag_rsem, fw_ssem, fw_rsem, v_ssem, v_rsem, k_sem, h_sem,
-           one_ssem, one_rsem, two_ssem, two_rsem, av_ssem, av_rsem, t_ssem, t_rsem, s_ssem, s_rsem, sf_ssem, sf_rsem, r_ssem, r_rsem, own_sem):
+           one_ssem, one_rsem, two_ssem, two_rsem, av_ssem, av_rsem, t_ssem, t_rsem, s_ssem, s_rsem, sf_ssem, sf_rsem, r_ssem, r_rsem, own_sem, ht_sem, refit_sem):
     e = lax.axis_index("expert")
     s = lax.axis_index("shard")
     p = s // 2
@@ -296,6 +296,9 @@
     h_copy = remote(hown, hsib, h_sem.at[0], h_sem.at[1], sib)
     h_copy.start()
     ht[...] = jnp.transpose(hown[...].astype(F32)).astype(BF16)
+    ht_copy = pltpu.make_async_copy(ht, ht_hbm, ht_sem)
+    ht_copy.start()
+    pending["ht"] = ht_copy.wait
 
     def grams(h, base):
         for f in range(2):
@@ -487,13 +490,16 @@
         s_in(k, q).wait_recv()
         sf_copy(k, q).start()
 
-    loop(1, CHIPS, share_step)
-
+    loop(1, 12, share_step)
     for back_copy in returns:
         back_copy.wait()
-    refit_ref[...] = lax.dot_general(combining, ret[...].astype(F32), (((0,), (0,)), ((), ())),
-                                     precision=lax.Precision.HIGHEST, preferred_element_type=F32).astype(BF16)
+    refitted[...] = lax.dot_general(combining, ret[...].astype(F32), (((0,), (0,)), ((), ())),
+                                    precision=lax.Precision.HIGHEST, preferred_element_type=F32).astype(BF16)
+    refit_copy = pltpu.make_async_copy(refitted, refit_hbm, refit_sem)
+    refit_copy.start()
+    loop(12, CHIPS, share_step)
     loop(0, CHIPS, lambda k: sf_wait(k, from_chip(k)))
+    refit_copy.wait()
     finish()
 
 
@@ -550,7 +556,7 @@
         out_shape=(jax.ShapeDtypeStruct((CHIPS, 2, 128, 128), BF16), jax.ShapeDtypeStruct((own, ROWS), BF16),
                    jax.ShapeDtypeStruct((rows, DW // SHARDS), BF16)),
         in_specs=[hbm] * 7,
-        out_specs=(hbm, vmem, vmem),
+        out_specs=(hbm, hbm, hbm),
         scratch_shapes=[
             pltpu.VMEM((rows, width), BF16),
             pltpu.VMEM((rows, direct), BF16),
@@ -568,6 +574,7 @@
             pltpu.VMEM((ROWS, own), F32),
             pltpu.VMEM((ROWS, own), BF16),
             pltpu.VMEM((ROWS, own), BF16),
+            pltpu.VMEM((own, ROWS), BF16),
             pltpu.VMEM((CHIPS, own, 128), BF16),
             pltpu.VMEM((2, SHARDS, 128), F32),
             pltpu.VMEM((2, SHARDS, 128), F32),
@@ -581,6 +588,7 @@
             pltpu.VMEM((ROWS, 128), BF16),
             pltpu.VMEM((ROWS, 128), BF16),
             pltpu.VMEM((ROWS, 128), BF16),
+            pltpu.VMEM((rows, DW // SHARDS), BF16),
             dma((8,)),
             dma((4,)), dma((4,)),
             dma((4,)), dma((4,)),
@@ -596,7 +604,7 @@
             dma((CHIPS,)), dma((CHIPS,)),
             dma((CHIPS,)), dma((CHIPS,)),
             dma((GROUPS,)), dma((GROUPS,)),
-            dma,
+            dma, dma, dma,
         ],
         compiler_params=pltpu.CompilerParams(collective_id=0, has_side_effects=True, vmem_limit_bytes=60 << 20),
         name="refit",

time: 66 us -> 65.3 us (0.989)
  no operation moved by 1% of the time
where the time goes in v5:
time: 65.3 us; the launch traced here: 65.2 us
  Pallas kernels  64.6 us (99%)
    pallas_call x1, Pallas kernels, body(): pl.pallas_call(kernel, out_shape=(jax.ShapeDtypeStruct((CHIPS, 2, 128, 12...  60.7 us
    pallas_call x1, Pallas kernels, body(): pl.pallas_call(apply_kernel, out_shape=(jax.ShapeDtypeStruct(refit.shape,...  3.86 us

profile of v5, /device:TPU:1, one launch (start us, length us, event | category | flops | bytes accessed | tf_op | source)
XLA Modules:
  0.0 65.2 jit_solution(1320003928689320544)
XLA Ops:
  0.6 60.7 %refit.1 = (bf16[16,2,128,128]{3,2,1,0:T(8,128)(2,1)}, bf16[256,128]{1,0:T(8,128)(2,1)}, bf16[32,128]{1,0:T(8,128)(2,1)}) custom-call(bf16[32,6144]{1,0:T(8,128)(2,1)} %tok_hbm.1, s32[2,32]{1,0:T(2,128)} %bitcast.2, f32[2,32]{1,0:T(2,128)} %bitcast.3, bf16[1,6144,256]{2,1,0:T(8,128)(2,1)} %gate_hbm.1, bf16[1,6144,256]{2,1,0:T(8,128)(2,1)} %up_hbm.1, ...), custom_call_target="tpu_custom_call" | custom-call | tf_op jit(solution)/shard_map/refit/pallas_call | solution.py:554
  61.4 3.9 %apply.1 = (bf16[32,128]{1,0:T(8,128)(2,1)}, bf16[1,256,4096]{2,1,0:T(8,128)(2,1)}) custom-call(bf16[16,2,128,128]{3,2,1,0:T(8,128)(2,1)} %get-tuple-element.5.sg_hbm, bf16[256,128]{1,0:T(8,128)(2,1)} %get-tuple-element.6.ht_hbm, bf16[32,128]{1,0:T(8,128)(2,1)} %get-tuple-element.7.refit_hbm, bf16[1,256,4096]{2,1,0:T(8,128)(2,1)} %down_hbm.3, ...), custom_call_target="tpu_custom_call" | custom-call | tf_op jit(solution)/shard_map/apply/pallas_call | solution.py:612
